TPU v7x, 32 devices: a whole 2x2x4 slice. The times are simulated.
32 devices in a mesh: cand: 2 (over y), gx: 4 (over z), gy: 2 (over x), wa: 2 (over core).
Axes of the slice: x: 2, y: 2, z: 4, core: 2. Of those that a mesh axis runs over, the one named last changes fastest.
Arguments:
- field: bfloat16 [4, 4, 2, 4, 4, 128, 128], P('wa', 'cand', None, 'gx', None, 'gy'), parts along dimension 1, may hold values from -6 to 6
- active_rows: int32 [4, 4], P('gx'), may hold values from 0 to 128, as said below
- kern: bfloat16 [4, 2, 4, 64, 128], P('wa'), may hold values from -0.25 to 0.25
- target: float32 [4, 64, 64], P('wa'), may hold values from 0 to 3
Outputs:
- design_grad: float32 [4, 8, 128, 128], P('gx', 'cand', 'gy'), parts along dimension 1
- intensity: float32 [4, 128, 64], P('wa', 'cand'), parts along dimension 1
There are 2 independent parts, one for each index of `cand`. A program takes and returns all parts, laid end to end along the dimension named above; an argument that names none is the same for every part. Nothing has to cross between parts.
Inputs may be any that keep to these rules, and one draw needn't show every extreme that they name: `active_rows`: live rows are counted from a tile's first cell row; tiles near the aperture's centre are full and its corners empty.
All inputs are finite; a program needn't handle non-finite values.
Results may differ from a plain program's by a relative error of at most 0.0075.
Values may be sent and summed in bfloat16 or wider, within the bound.
No kernel may reach another device: no remote copies, remote signals or barrier semaphores. Data moves between devices by JAX's collectives and lax.ppermute only.
A program may use at most 128 MiB of HBM per device.

v0:
```python
import functools

import jax
import jax.numpy as jnp
from jax import lax
from jax.experimental import pallas as pl
from jax.experimental.pallas import tpu as pltpu
from jax.sharding import PartitionSpec as P

VMEM = 16 * 2**20


def two_terms(value):
    high = value.astype(jnp.bfloat16)
    return high, (value - high.astype(jnp.float32)).astype(jnp.bfloat16)


def dot(first, second, over):
    return lax.dot_general(
        first, second, ((over[:1], over[1:]), ((), ())), preferred_element_type=jnp.float32
    )


def swapped(value, focus, left, right):
    lane = lax.broadcasted_iota(jnp.int32, value.shape, 1)
    sign = jnp.where(lane < focus, jnp.float32(left), jnp.float32(right))
    return pltpu.roll(value, focus, 1) * sign


def tile_kern(kern, wave, tile):
    real, imag = kern[wave, 0, tile], kern[wave, 1, tile]
    return jnp.concatenate([real, imag], axis=0), jnp.concatenate([-imag, real], axis=0)


def in_block(shape, block, width):
    lane = lax.broadcasted_iota(jnp.int32, shape, len(shape) - 1)
    return (lane >= block * width) & (lane < (block + 1) * width)


def side_by_side(first, second, block, blocks):
    width = first.shape[-1] // blocks
    first, second = first.astype(jnp.float32), second.astype(jnp.float32)
    beside = in_block(first.shape, lax.rem(block + 1, blocks), width)
    moved = jnp.where(beside, pltpu.roll(second, width, first.ndim - 1), 0.0)
    return jnp.where(in_block(first.shape, block, width), first, moved).astype(jnp.bfloat16)


def over_tiles(tiles, body, init):
    return lax.fori_loop(0, tiles, body, init, unroll=tiles <= 8)


def live_rows(count, shape):
    height = shape[-2]
    row = lax.axis_index("gy") * height + lax.broadcasted_iota(jnp.int32, shape, len(shape) - 2)
    return row < count


def share_kernel(rows_far, field_far, kern_far, share, field, kern, counts, rows, spread, arrived):
    waves, polars, _, tiles, height, side = field.shape
    focus = kern.shape[3]
    copies = [pltpu.make_async_copy(rows_far, rows, arrived.at[2 * waves])]
    for wave in range(waves):
        copies += [
            pltpu.make_async_copy(kern_far.at[wave], kern.at[wave], arrived.at[2 * wave]),
            pltpu.make_async_copy(
                field_far.at[wave, :, :, 0], field.at[wave], arrived.at[2 * wave + 1]
            ),
        ]
    for copy in copies:
        copy.start()
    tile_row = lax.axis_index("gx")
    first = pl.multiple_of(lax.axis_index("gy") * height, height)
    spread[...] = jnp.zeros_like(spread)
    copies[0].wait()
    inner = []
    for wave in range(waves):
        copies[2 * wave + 1].wait()
        copies[2 * wave + 2].wait()

        def add_tile(tile, value):
            live = live_rows(rows[0, tile], (polars, height, side))
            planes = [
                jnp.where(live, field[wave, :, part, tile], jnp.zeros((), field.dtype))
                for part in range(2)
            ]
            planes = [plane.reshape(polars * height, side) for plane in planes]
            return value + dot(
                jnp.concatenate(planes, axis=1),
                jnp.concatenate(tile_kern(kern, wave, tile), axis=1),
                (1, 1),
            )

        zero = jnp.zeros((polars * height, 2 * focus), jnp.float32)
        inner.append(over_tiles(tiles, add_tile, zero))
    for wave in range(waves):
        for polar in range(polars):
            lanes = pl.ds(polar * 2 * focus, 2 * focus)
            terms = two_terms(inner[wave][polar * height : (polar + 1) * height])
            for index, term in enumerate(terms):
                spread[wave, pl.ds(index * side + first, height), lanes] = term
        own = tile_kern(kern, wave, tile_row)[0]
        both = dot(jnp.concatenate([own, own], axis=1), spread[wave], (1, 0))
        for polar in range(polars):
            lanes = slice(polar * 2 * focus, (polar + 1) * 2 * focus)
            straight, crossed = both[:focus, lanes], both[focus:, lanes]
            share[wave, polar] = (straight + swapped(crossed, focus, -1, 1)).astype(share.dtype)

    def put_count(tile, carry):
        counts[tile] = jnp.full(counts.shape[1:], rows[0, tile], jnp.int32)
        return carry

    over_tiles(tiles, put_count, 0)


def strip_kernel(field, kern, counts, own_kern, both_kern, strip_kern, *strips):
    waves, polars, _, tiles, height, side = field.shape
    blocks = side // height
    block = lax.axis_index("gy")
    tile_row = lax.axis_index("gx")
    for wave in range(waves):
        for part in range(2):
            turned = kern[wave, part, tile_row].astype(jnp.float32).T.astype(kern.dtype)
            own_kern[wave, pl.ds(part * side, side)] = jnp.concatenate([turned, turned], axis=1)

    def one_tile(tile, carry):
        live = live_rows(counts[tile, :1], (height, side))
        for wave in range(waves):
            parts = tile_kern(kern, wave, tile)
            both_kern[wave, tile] = jnp.concatenate(parts, axis=1)
            strip_kern[wave, tile] = side_by_side(*parts, block, blocks)
            for polar in range(polars):
                for distance, strip in enumerate(strips):
                    both = side_by_side(
                        field[wave, polar, 0, tile],
                        field[wave, polar, 1, tile],
                        block ^ distance,
                        blocks,
                    )
                    strip[wave, polar, tile] = jnp.where(live, both, jnp.zeros((), both.dtype))
        return carry

    over_tiles(tiles, one_tile, 0)


def twice(value):
    return jnp.concatenate([value, value], axis=0)


def crossed_kernel(scale, blocks, own_kern, strip_kern, target, *refs):
    strips, refs = refs[:blocks], refs[blocks:]
    shares, (powers, sides, crossed, rowside, whole, turned) = refs[:-6], refs[-6:]
    waves, polars, tiles, height, side = strips[0].shape
    focus = target.shape[1]
    block = lax.axis_index("gy")
    for wave in range(waves):
        focal = [
            total([share[wave, polar].astype(jnp.float32) for share in shares])
            for polar in range(polars)
        ]
        power = sum(value * value for value in focal)
        powers[wave] = power
        power = power + pltpu.roll(power, focus, 1)
        goal = target[wave]
        excess = power - jnp.concatenate([goal, goal], axis=1)
        source = jnp.concatenate([excess * value for value in focal], axis=1)
        terms = jnp.concatenate(two_terms(source), axis=0)
        rowside[wave] = dot(own_kern[wave], terms, (1, 0))
    near = []
    for wave in range(waves):
        near.append([])
        for distance in range(blocks):
            first = pl.multiple_of((block ^ distance) * height, height)
            parts = []
            for polar in range(polars):
                lanes = pl.ds(polar * 2 * focus, 2 * focus)
                straight = rowside[wave, pl.ds(first, height), lanes]
                across = rowside[wave, pl.ds(side + first, height), lanes]
                parts.append(straight + swapped(across, focus, 1, -1))
            terms = two_terms(jnp.concatenate(parts, axis=0))
            near[wave].append(jnp.concatenate(terms, axis=1))
        sides[wave] = near[wave][0]

    def add_tile(distance, carry):
        tile = lax.axis_index("gx") ^ distance
        for index, strip in enumerate(strips):
            value = jnp.zeros((height, side), jnp.float32)
            for wave in range(waves):
                back = dot(near[wave][index], twice(strip_kern[wave, tile]), (1, 0))
                back = back.reshape(polars, height, side)
                for polar in range(polars):
                    value += back[polar] * strip[wave, polar, tile].astype(jnp.float32)
            first = pl.multiple_of((block ^ index) * height, height)
            whole[distance, pl.ds(first, height)] = (
                value + pltpu.roll(value, side - height, 1)
            ) * scale
        turned[distance] = whole[distance].T
        own = turned[distance, pl.ds(pl.multiple_of(block * height, height), height)]
        crossed[distance] = own.astype(crossed.dtype)
        return carry

    over_tiles(tiles, add_tile, 0)


def straight_kernel(scale, field, counts, both_kern, sides, gradient):
    waves, polars, _, tiles, height, side = field.shape

    def add_tile(distance, carry):
        tile = lax.axis_index("gx") ^ distance
        term = jnp.zeros((height, side), jnp.float32)
        for wave in range(waves):
            back = dot(sides[wave], twice(both_kern[wave, tile]), (1, 0))
            back = back.reshape(polars, height, 2 * side)
            for polar in range(polars):
                for part in range(2):
                    plane = field[wave, polar, part, tile].astype(jnp.float32)
                    term += back[polar, :, part * side : (part + 1) * side] * plane
        live = live_rows(counts[tile, :1], (height, side))
        gradient[distance] = jnp.where(live, term * scale, 0.0)
        return carry

    over_tiles(tiles, add_tile, 0)


def call(kernel, out_shape, scratch, args, spaces):
    return pl.pallas_call(
        kernel,
        out_shape=out_shape,
        in_specs=[pl.BlockSpec(memory_space=space) for space in spaces],
        out_specs=[pl.BlockSpec(memory_space=pltpu.VMEM)] * len(out_shape),
        scratch_shapes=scratch,
        compiler_params=pltpu.CompilerParams(vmem_limit_bytes=VMEM),
    )(*args)


def pairs(count, distance):
    return [(device, device ^ distance) for device in range(count)]


def partners(value, axis, count):
    came = {d: lax.ppermute(value(d), axis, pairs(count, d)) for d in range(count - 1, 0, -1)}
    return [came[d] for d in range(1, count)]


def crosswise(value, mesh):
    count, cores = mesh.shape["gx"], mesh.shape["wa"]

    def routes(distance):
        odd = distance % 2 == 1
        return [
            (
                device * cores + core,
                (device ^ distance) * cores + (cores - 1 - core if odd else core),
            )
            for device in range(count)
            for core in range(cores)
        ]

    came = {d: lax.ppermute(value(d), ("gx", "wa"), routes(d)) for d in range(count - 1, 0, -1)}
    return [came[d] for d in range(1, count)]


def total(terms):
    while len(terms) > 1:
        terms = [first + second for first, second in zip(terms[::2], terms[1::2])]
    return terms[0]


def rounded(value):
    return lax.reduce_precision(value, 8, 7)


def in_order(came, me):
    count = came.shape[0]
    rest = came.shape[1:]
    bit = 1
    while bit < count:
        split = came.reshape((count // (2 * bit), 2, bit) + rest)
        came = jnp.where((me & bit) != 0, split[:, ::-1], split).reshape((count,) + rest)
        bit *= 2
    return came


def make(mesh):
    count_x = mesh.shape["gx"]
    count_y = mesh.shape["gy"]

    def on_device(field, active_rows, kern, target):
        tile_row = lax.axis_index("gx")
        waves, polars = field.shape[0], field.shape[1]
        tiles = field.shape[4]
        rows_dev = field.shape[5]
        side = field.shape[6]
        focus = kern.shape[3]
        shape = (waves, polars, focus, 2 * focus)
        share, near_field, near_kern, counts = call(
            share_kernel,
            [
                jax.ShapeDtypeStruct(shape, jnp.bfloat16),
                jax.ShapeDtypeStruct(field.shape[:3] + field.shape[4:], field.dtype),
                jax.ShapeDtypeStruct(kern.shape, kern.dtype),
                jax.ShapeDtypeStruct((tiles, 8, side), jnp.int32),
            ],
            [
                pltpu.SMEM(active_rows.shape, jnp.int32),
                pltpu.VMEM((waves, 2 * side, polars * 2 * focus), jnp.bfloat16),
                pltpu.SemaphoreType.DMA((2 * waves + 1,)),
            ],
            [
                pltpu.with_memory_space_constraint(operand, pltpu.HBM)
                for operand in (active_rows, field, kern)
            ],
            [pltpu.HBM] * 3,
        )
        shares = [share] + partners(lambda d: share, "gy", count_y)
        share = total([term.astype(jnp.float32) for term in shares]).astype(jnp.bfloat16)
        strip_shape = (waves, polars, tiles, rows_dev, side)
        own_kern, both_kern, strip_kern, own_strip, *strips = call(
            strip_kernel,
            [
                jax.ShapeDtypeStruct((waves, 2 * side, 2 * focus), kern.dtype),
                jax.ShapeDtypeStruct((waves, tiles, 2 * focus, 2 * side), kern.dtype),
                jax.ShapeDtypeStruct((waves, tiles, 2 * focus, side), kern.dtype),
            ]
            + [jax.ShapeDtypeStruct(strip_shape, field.dtype)] * count_y,
            [],
            (near_field, near_kern, counts),
            [pltpu.VMEM] * 3,
        )
        strips = partners(lambda d: strips[d - 1], "gy", count_y)
        shares = [share] + partners(lambda d: share, "gx", count_x)
        shares = shares[::-1]
        shape = (tiles, rows_dev, side)
        scale = tiles * side / focus
        powers, sides, crossed = call(
            functools.partial(crossed_kernel, scale, count_y),
            [
                jax.ShapeDtypeStruct((waves, focus, 2 * focus), jnp.float32),
                jax.ShapeDtypeStruct((waves, polars * rows_dev, 4 * focus), jnp.bfloat16),
                jax.ShapeDtypeStruct(shape, jnp.bfloat16),
            ],
            [pltpu.VMEM((waves, 2 * side, polars * 2 * focus), jnp.float32)]
            + [pltpu.VMEM((tiles, side, side), jnp.float32)] * 2,
            (own_kern, strip_kern, target, own_strip, *strips, *shares),
            [pltpu.VMEM] * (3 + count_x + count_y),
        )
        (gradient,) = call(
            functools.partial(straight_kernel, scale),
            [jax.ShapeDtypeStruct(shape, jnp.float32)],
            [],
            (near_field, counts, both_kern, sides),
            [pltpu.VMEM] * 4,
        )
        came = [crossed[0]] + crosswise(lambda d: crossed[d], mesh)
        own = rounded(gradient + jnp.stack(came).astype(jnp.float32))
        other = lax.ppermute(own.astype(jnp.bfloat16), "wa", pairs(2, 1))
        design_grad = in_order(0.5 * (own + other.astype(jnp.float32)), tile_row)
        intensity = powers[:, :, :focus] + powers[:, :, focus:]
        return (design_grad[None], intensity)

    return on_device


def solution(mesh):
    placed = (
        P("wa", "cand", None, "gx", None, "gy", None),
        P("gx", None),
        P("wa", None, None, None, None),
        P("wa", None, None),
    )
    return jax.shard_map(
        make(mesh),
        mesh=mesh,
        in_specs=placed,
        out_specs=(P("gx", "cand", "gy", None), P("wa", "cand", None)),
        check_vma=False,
    )
```

profile of v0, /device:TPU:0, one launch (start us, length us, event | category | flops | bytes accessed | tf_op | source)
XLA Modules:
  0.0 25.9 jit_solution(15605786347451937743)
XLA Ops:
  0.6 1.9 %shard_map.59 = (bf16[2,2,64,128]{3,2,1,0:T(8,128)(2,1)S(1)}, bf16[2,2,2,4,64,128]{5,4,3,2,1,0:T(8,128)(2,1)S(1)}, bf16[2,2,4,64,128]{4,3,2,1,0:T(8,128)(2,1)S(1)}, s32[4,8,128]{2,1,0:T(8,128)S(1)}) custom-call(s32[1,4]{1,0:T(1,128)} %rows_far.1, bf16[2,2,2,1,4,64,128]{6,5,4,3,2,1,0:T(8,128)(2,1)} %field_far.1, bf16[2,2,4,64,128]{4,3,2,1,0:T(8,128)(2,1)} %kern_far.1), custom_call_target="tpu_custom_call" | custom-call | tf_op jit(solution)/shard_map/pallas_call | solution.py:225
  2.5 3.0 %collective-permute-start.1 = (bf16[2,2,64,128]{3,2,1,0:T(8,128)(2,1)S(1)}, bf16[2,2,64,128]{3,2,1,0:T(8,128)(2,1)S(1)}, u32[]{:S(2)}, u32[]{:S(2)}) collective-permute-start(bf16[2,2,64,128]{3,2,1,0:T(8,128)(2,1)S(1)} %get-tuple-element.22), channel_id=1, source_target_pairs={{0,2},{2,0},{1,3},{3,1},{4,6},{6,4},{5,7},{7,5},{8,10},{10,8},{9,1... | collective-permute-start | bytes 196616 | tf_op jit(solution)/shard_map/ppermute | solution.py:240
  5.5 0.5 %shard_map.60 = (bf16[2,256,128]{2,1,0:T(8,128)(2,1)S(1)}, bf16[2,4,128,256]{3,2,1,0:T(8,128)(2,1)S(1)}, bf16[2,4,128,128]{3,2,1,0:T(8,128)(2,1)S(1)}, bf16[2,2,...) custom-call(bf16[2,2,2,4,64,128]{5,4,3,2,1,0:T(8,128)(2,1)S(1)} %get-tuple-element.14.field, ...), custom_call_target="tpu_custom_call" | custom-call | tf_op jit(solution)/shard_map/pallas_call | solution.py:225
  6.0 0.0 copy-start
  6.1 0.1 collective-permute-start
  6.1 1.9 %collective-permute-done.1 = bf16[2,2,64,128]{3,2,1,0:T(8,128)(2,1)S(1)} collective-permute-done((bf16[2,2,64,128]{3,2,1,0:T(8,128)(2,1)S(1)}, bf16[2,2,64,128]{3,2,1,0:T(8,128)(2,1)S(1)}, u32[]{:S(2)}, u32[]{:S(2)}) %collective-permute-start.1) | collective-permute-done | bytes 65568 | tf_op jit(solution)/shard_map/ppermute | solution.py:240
  8.1 4.0 %collective-permute-start.2 = (bf16[2,2,64,128]{3,2,1,0:T(8,128)(2,1)S(1)}, bf16[2,2,64,128]{3,2,1,0:T(8,128)(2,1)S(1)}, u32[]{:S(2)}, u32[]{:S(2)}) collective-permute-start(bf16[2,2,64,128]{3,2,1,0:T(8,128)(2,1)S(1)} %add_convert_fusion.refs_5_), channel_id=1, source_target_pairs={{0,12},{4,8},{8,4},{12,0},{1,13},{5,9},{9,5},{13,1},{2,14},{6,10},... | collective-permute-start | bytes 196616 | tf_op jit(solution)/shard_map/ppermute | solution.py:240
  12.1 0.0 collective-permute-start.3
  12.1 0.6 %collective-permute-start.4 = (bf16[2,2,64,128]{3,2,1,0:T(8,128)(2,1)S(1)}, bf16[2,2,64,128]{3,2,1,0:T(8,128)(2,1)S(1)}, u32[]{:S(2)}, u32[]{:S(2)}) collective-permute-start(bf16[2,2,64,128]{3,2,1,0:T(8,128)(2,1)S(1)} %add_convert_fusion.refs_5_), channel_id=1, source_target_pairs={{0,4},{4,0},{8,12},{12,8},{1,5},{5,1},{9,13},{13,9},{2,6},{6,2},{1... | collective-permute-start | bytes 196616 | tf_op jit(solution)/shard_map/ppermute | solution.py:240
  12.8 1.7 %collective-permute-done.2.refs_2_ = bf16[2,2,64,128]{3,2,1,0:T(8,128)(2,1)S(1)} collective-permute-done((bf16[2,2,64,128]{3,2,1,0:T(8,128)(2,1)S(1)}, bf16[2,2,64,128]{3,2,1,0:T(8,128)(2,1)S(1)}, u32[]{:S(2)}, u32[]{:S(2)}) %collective-permute-start.2) | collective-permute-done | bytes 65568 | tf_op jit(solution)/shard_map/ppermute | solution.py:240
  14.4 2.8 %collective-permute-done.3.refs_3_ = bf16[2,2,64,128]{3,2,1,0:T(8,128)(2,1)S(1)} collective-permute-done((bf16[2,2,64,128]{3,2,1,0:T(8,128)(2,1)S(1)}, bf16[2,2,64,128]{3,2,1,0:T(8,128)(2,1)S(1)}, u32[]{:S(2)}, u32[]{:S(2)}) %collective-permute-start.3) | collective-permute-done | bytes 65568 | tf_op jit(solution)/shard_map/ppermute | solution.py:240
  17.3 0.0 collective-permute-done.4.refs_4_
  17.3 0.0 collective-permute-done.refs_1_
  17.3 0.0 copy-done
  17.3 1.0 %shard_map.61 = (f32[2,64,128]{2,1,0:T(8,128)S(1)}, bf16[2,128,256]{2,1,0:T(8,128)(2,1)S(1)}, bf16[4,64,128]{2,1,0:T(8,128)(2,1)S(1)}) custom-call(bf16[2,256,128]{2,1,0:T(8,128)(2,1)S(1)} %get-tuple-element.18.own_kern, bf16[2,4,128,128]{3,2,1,0:T(8,128)(2,1)S(1)} %get-tuple-element.19.strip_kern, f32[2,64,64]{2,1,0:T(8,128)S(1)} %copy-done, ...), custom_call_target="tpu_custom_call" | custom-call | tf_op jit(solution)/shard_map/pallas_call | solution.py:225
  18.3 0.1 collective-permute-start.7
  18.4 2.1 %collective-permute-start.6 = (bf16[64,128]{1,0:T(8,128)(2,1)S(1)}, bf16[64,128]{1,0:T(8,128)(2,1)S(1)}, u32[]{:S(2)}, u32[]{:S(2)}) collective-permute-start(bf16[64,128]{1,0:T(8,128)(2,1)S(1)} %get-tuple-element.28), channel_id=1, source_target_pairs={{0,8},{1,9},{4,12},{5,13},{8,0},{9,1},{12,4},{13,5},{2,10},{3,11},... | collective-permute-start | bytes 49160 | tf_op jit(solution)/shard_map/ppermute | solution.py:258
  20.5 1.7 %collective-permute-start.5 = (bf16[64,128]{1,0:T(8,128)(2,1)S(1)}, bf16[64,128]{1,0:T(8,128)(2,1)S(1)}, u32[]{:S(2)}, u32[]{:S(2)}) collective-permute-start(bf16[64,128]{1,0:T(8,128)(2,1)S(1)} %get-tuple-element.29), channel_id=1, source_target_pairs={{0,5},{1,4},{4,1},{5,0},{8,13},{9,12},{12,9},{13,8},{2,7},{3,6},{6... | collective-permute-start | bytes 49160 | tf_op jit(solution)/shard_map/ppermute | solution.py:258
  22.2 0.3 %shard_map.62 = f32[4,64,128]{2,1,0:T(8,128)S(1)} custom-call(bf16[2,2,2,4,64,128]{5,4,3,2,1,0:T(8,128)(2,1)S(1)} %get-tuple-element.14.field, s32[4,8,128]{2,1,0:T(8,128)S(1)} %get-tuple-element.15.counts, bf16[2,4,128,256]{3,2,1,0:T(8,128)(2,1)S(1)} %get-tuple-element.17.both_kern, bf16[2,128,256]{2,1,0:T(8,128)(2,1)S(1)} %get-tuple-element.23.sides), custom_call_target="tpu_custom_call" | custom-call | tf_op jit(solution)/shard_map/pallas_call | solution.py:225
  22.5 0.8 %collective-permute-done.7 = bf16[64,128]{1,0:T(8,128)(2,1)S(1)} collective-permute-done((bf16[64,128]{1,0:T(8,128)(2,1)S(1)}, bf16[64,128]{1,0:T(8,128)(2,1)S(1)}, u32[]{:S(2)}, u32[]{:S(2)}) %collective-permute-start.7) | collective-permute-done | bytes 16416 | tf_op jit(solution)/shard_map/ppermute | solution.py:258
  23.3 0.1 collective-permute-done.6
  23.4 0.2 collective-permute-done.5
  23.7 0.6 %collective-permute-start.8 = (bf16[4,64,128]{2,1,0:T(8,128)(2,1)S(1)}, bf16[4,64,128]{2,1,0:T(8,128)(2,1)S(1)}, u32[]{:S(2)}, u32[]{:S(2)}) collective-permute-start(bf16[4,64,128]{2,1,0:T(8,128)(2,1)S(1)} %fusion.1), channel_id=1, source_target_pairs={{0,1},{1,0},{2,3},{3,2},{4,5},{5,4},{6,7},{7,6},{8,9},{9,8},{10,11... | collective-permute-start | bytes 196616 | tf_op jit(solution)/shard_map/ppermute | solution.py:355
  24.3 0.7 %slice_add_fusion = f32[2,64,64]{2,1,0:T(8,128)} fusion(f32[2,64,128]{2,1,0:T(8,128)S(1)} %get-tuple-element.25), kind=kLoop, calls=%fused_computation.8 | loop fusion | flops 8192 | bytes 98304 | tf_op jit(solution)/shard_map/add | solution.py:357
  25.0 0.2 collective-permute-done.8
  25.2 0.7 %reverse_select_fusion = f32[1,2,2,64,128]{4,3,2,1,0:T(8,128)} fusion(f32[1,2,2,64,128]{4,3,2,1,0:T(8,128)S(1)} %fusion, pred[]{:T(512)S(6)} %ne.6), kind=kLoop, calls=%fused_computation | loop fusion | flops 32768 | bytes 262145 | tf_op jit(solution)/shard_map/jit(_where)/select_n | solution.py:278
  (5 shorter events, 0.1 us)
Async XLA Ops:
  2.5 5.5 %collective-permute-start.1 = (bf16[2,2,64,128]{3,2,1,0:T(8,128)(2,1)S(1)}, bf16[2,2,64,128]{3,2,1,0:T(8,128)(2,1)S(1)}, u32[]{:S(2)}, u32[]{:S(2)}) collective-permute-start(bf16[2,2,64,128]{3,2,1,0:T(8,128)(2,1)S(1)} %get-tuple-element.22), channel_id=1, source_target_pairs={{0,2},{2,0},{1,3},{3,1},{4,6},{6,4},{5,7},{7,5},{8,10},{10,8},{9,1... | collective-permute-start | bytes 196616 | tf_op jit(solution)/shard_map/ppermute | solution.py:240
  6.0 11.2 %copy-start = (f32[2,64,64]{2,1,0:T(8,128)S(1)}, f32[2,64,64]{2,1,0:T(8,128)}, u32[]{:S(2)}) copy-start(f32[2,64,64]{2,1,0:T(8,128)} %target.1) | copy-start | bytes 98308
  6.1 11.2 %collective-permute-start = (bf16[2,2,4,64,128]{4,3,2,1,0:T(8,128)(2,1)S(1)}, bf16[2,2,4,64,128]{4,3,2,1,0:T(8,128)(2,1)S(1)}, u32[]{:S(2)}, u32[]{:S(2)}) collective-permute-start(bf16[2,2,4,64,128]{4,3,2,1,0:T(8,128)(2,1)S(1)} %get-tuple-element.21), channel_id=1, source_target_pairs={{0,2},{2,0},{1,3},{3,1},{4,6},{6,4},{5,7},{7,5},{8,10},{10,8},{9,1... | collective-permute-start | bytes 786440 | tf_op jit(solution)/shard_map/ppermute | solution.py:240
  8.1 6.4 %collective-permute-start.2 = (bf16[2,2,64,128]{3,2,1,0:T(8,128)(2,1)S(1)}, bf16[2,2,64,128]{3,2,1,0:T(8,128)(2,1)S(1)}, u32[]{:S(2)}, u32[]{:S(2)}) collective-permute-start(bf16[2,2,64,128]{3,2,1,0:T(8,128)(2,1)S(1)} %add_convert_fusion.refs_5_), channel_id=1, source_target_pairs={{0,12},{4,8},{8,4},{12,0},{1,13},{5,9},{9,5},{13,1},{2,14},{6,10},... | collective-permute-start | bytes 196616 | tf_op jit(solution)/shard_map/ppermute | solution.py:240
  12.1 5.2 %collective-permute-start.3 = (bf16[2,2,64,128]{3,2,1,0:T(8,128)(2,1)S(1)}, bf16[2,2,64,128]{3,2,1,0:T(8,128)(2,1)S(1)}, u32[]{:S(2)}, u32[]{:S(2)}) collective-permute-start(bf16[2,2,64,128]{3,2,1,0:T(8,128)(2,1)S(1)} %add_convert_fusion.refs_5_), channel_id=1, source_target_pairs={{0,8},{4,12},{8,0},{12,4},{1,9},{5,13},{9,1},{13,5},{2,10},{6,14},... | collective-permute-start | bytes 196616 | tf_op jit(solution)/shard_map/ppermute | solution.py:240
  12.1 5.2 %collective-permute-start.4 = (bf16[2,2,64,128]{3,2,1,0:T(8,128)(2,1)S(1)}, bf16[2,2,64,128]{3,2,1,0:T(8,128)(2,1)S(1)}, u32[]{:S(2)}, u32[]{:S(2)}) collective-permute-start(bf16[2,2,64,128]{3,2,1,0:T(8,128)(2,1)S(1)} %add_convert_fusion.refs_5_), channel_id=1, source_target_pairs={{0,4},{4,0},{8,12},{12,8},{1,5},{5,1},{9,13},{13,9},{2,6},{6,2},{1... | collective-permute-start | bytes 196616 | tf_op jit(solution)/shard_map/ppermute | solution.py:240
  18.3 5.0 %collective-permute-start.7 = (bf16[64,128]{1,0:T(8,128)(2,1)S(1)}, bf16[64,128]{1,0:T(8,128)(2,1)S(1)}, u32[]{:S(2)}, u32[]{:S(2)}) collective-permute-start(bf16[64,128]{1,0:T(8,128)(2,1)S(1)} %get-tuple-element.27), channel_id=1, source_target_pairs={{0,13},{1,12},{4,9},{5,8},{8,5},{9,4},{12,1},{13,0},{2,15},{3,14},... | collective-permute-start | bytes 49160 | tf_op jit(solution)/shard_map/ppermute | solution.py:258
  18.4 5.0 %collective-permute-start.6 = (bf16[64,128]{1,0:T(8,128)(2,1)S(1)}, bf16[64,128]{1,0:T(8,128)(2,1)S(1)}, u32[]{:S(2)}, u32[]{:S(2)}) collective-permute-start(bf16[64,128]{1,0:T(8,128)(2,1)S(1)} %get-tuple-element.28), channel_id=1, source_target_pairs={{0,8},{1,9},{4,12},{5,13},{8,0},{9,1},{12,4},{13,5},{2,10},{3,11},... | collective-permute-start | bytes 49160 | tf_op jit(solution)/shard_map/ppermute | solution.py:258
  20.5 3.2 %collective-permute-start.5 = (bf16[64,128]{1,0:T(8,128)(2,1)S(1)}, bf16[64,128]{1,0:T(8,128)(2,1)S(1)}, u32[]{:S(2)}, u32[]{:S(2)}) collective-permute-start(bf16[64,128]{1,0:T(8,128)(2,1)S(1)} %get-tuple-element.29), channel_id=1, source_target_pairs={{0,5},{1,4},{4,1},{5,0},{8,13},{9,12},{12,9},{13,8},{2,7},{3,6},{6... | collective-permute-start | bytes 49160 | tf_op jit(solution)/shard_map/ppermute | solution.py:258
  23.7 1.5 %collective-permute-start.8 = (bf16[4,64,128]{2,1,0:T(8,128)(2,1)S(1)}, bf16[4,64,128]{2,1,0:T(8,128)(2,1)S(1)}, u32[]{:S(2)}, u32[]{:S(2)}) collective-permute-start(bf16[4,64,128]{2,1,0:T(8,128)(2,1)S(1)} %fusion.1), channel_id=1, source_target_pairs={{0,1},{1,0},{2,3},{3,2},{4,5},{5,4},{6,7},{7,6},{8,9},{9,8},{10,11... | collective-permute-start | bytes 196616 | tf_op jit(solution)/shard_map/ppermute | solution.py:355
where the time goes:
time: 26 us; the launch traced here: 25.9 us
  starting transfers between devices  12.3 us (47%)
  waiting for transfers between devices  7.73 us (30%)
  Pallas kernels  3.71 us (14%)
  other arithmetic  1.47 us (6%)
  between operations  0.71 us (3%)
    ppermute x5, starting transfers between devices, partners(): lax.ppermute(value(d), axis, pairs(count, d))  7.78 us
    ppermute x5, waiting for transfers between devices, partners(): lax.ppermute(value(d), axis, pairs(count, d))  6.42 us
    ppermute x3, starting transfers between devices, crosswise(): lax.ppermute(value(d), ('gx', 'wa'), routes(d))  3.89 us
    pallas_call x4, Pallas kernels, call(): pl.pallas_call(kernel, out_shape=out_shape, in_specs=[pl.BlockSpec(memory...  3.71 us
    ppermute x3, waiting for transfers between devices, crosswise(): lax.ppermute(value(d), ('gx', 'wa'), routes(d))  1.12 us
    add x1, other arithmetic, on_device(): intensity = powers[:, :, :focus] + powers[:, :, focus:]  0.72 us
    select_n x1, other arithmetic, in_order(): jnp.where(me & bit != 0, split[:, ::-1], split).reshape((count,) + rest)  0.67 us
    ppermute x1, starting transfers between devices, on_device(): other = lax.ppermute(own.astype(jnp.bfloat16), 'wa', pairs(2, 1))  0.6 us
  transfers between devices with their start and end apart: 9, of which 7 were waited for; matrix products, arithmetic and copies ran while one was open for 3% of the time, Pallas kernels for 3%

commit v1 on v0

--- a/solution.py
+++ b/solution.py
@@ -148,7 +148,7 @@
 
 def crossed_kernel(scale, blocks, own_kern, strip_kern, target, *refs):
     strips, refs = refs[:blocks], refs[blocks:]
-    shares, (powers, sides, crossed, rowside, whole, turned) = refs[:-6], refs[-6:]
+    shares, (powers, sides, crossed, rowside, whole) = refs[:-5], refs[-5:]
     waves, polars, tiles, height, side = strips[0].shape
     focus = target.shape[1]
     block = lax.axis_index("gy")
@@ -180,6 +180,10 @@
             near[wave].append(jnp.concatenate(terms, axis=1))
         sides[wave] = near[wave][0]
 
+    lane = lax.broadcasted_iota(jnp.int32, (height, side), 1)
+    row = lax.broadcasted_iota(jnp.int32, (height, side), 0)
+    pick = jnp.where(lane == row + block * height, 1.0, 0.0).astype(whole.dtype)
+
     def add_tile(distance, carry):
         tile = lax.axis_index("gx") ^ distance
         for index, strip in enumerate(strips):
@@ -190,12 +194,9 @@
                 for polar in range(polars):
                     value += back[polar] * strip[wave, polar, tile].astype(jnp.float32)
             first = pl.multiple_of((block ^ index) * height, height)
-            whole[distance, pl.ds(first, height)] = (
-                value + pltpu.roll(value, side - height, 1)
-            ) * scale
-        turned[distance] = whole[distance].T
-        own = turned[distance, pl.ds(pl.multiple_of(block * height, height), height)]
-        crossed[distance] = own.astype(crossed.dtype)
+            value = (value + pltpu.roll(value, side - height, 1)) * scale
+            whole[distance, pl.ds(first, height)] = value.astype(whole.dtype)
+        crossed[distance] = dot(pick, whole[distance], (1, 1)).astype(crossed.dtype)
         return carry
 
     over_tiles(tiles, add_tile, 0)
@@ -339,7 +340,7 @@
                 jax.ShapeDtypeStruct(shape, jnp.bfloat16),
             ],
             [pltpu.VMEM((waves, 2 * side, polars * 2 * focus), jnp.float32)]
-            + [pltpu.VMEM((tiles, side, side), jnp.float32)] * 2,
+            + [pltpu.VMEM((tiles, side, side), jnp.bfloat16)],
             (own_kern, strip_kern, target, own_strip, *strips, *shares),
             [pltpu.VMEM] * (3 + count_x + count_y),
         )

time: 26 us -> 26.8 us (1.031)
  Pallas kernels: 3.71 us -> 4.45 us
    pallas_call x4, Pallas kernels: 3.71 us -> 4.45 us  [call(): pl.pallas_call(kernel, out_shape=out_shape, in_specs=[pl.BlockSpec(memory...]
where the time goes in v1:
time: 26.8 us; the launch traced here: 26.7 us
  starting transfers between devices  12.3 us (46%)
  waiting for transfers between devices  7.72 us (29%)
  Pallas kernels  4.45 us (17%)
  other arithmetic  1.47 us (5%)
  between operations  0.71 us (3%)
    ppermute x5, starting transfers between devices, partners(): lax.ppermute(value(d), axis, pairs(count, d))  7.78 us
    ppermute x5, waiting for transfers between devices, partners(): lax.ppermute(value(d), axis, pairs(count, d))  6.42 us
    pallas_call x4, Pallas kernels, call(): pl.pallas_call(kernel, out_shape=out_shape, in_specs=[pl.BlockSpec(memory...  4.45 us
    ppermute x3, starting transfers between devices, crosswise(): lax.ppermute(value(d), ('gx', 'wa'), routes(d))  3.89 us
    ppermute x3, waiting for transfers between devices, crosswise(): lax.ppermute(value(d), ('gx', 'wa'), routes(d))  1.11 us
    add x1, other arithmetic, on_device(): intensity = powers[:, :, :focus] + powers[:, :, focus:]  0.72 us
    select_n x1, other arithmetic, in_order(): jnp.where(me & bit != 0, split[:, ::-1], split).reshape((count,) + rest)  0.67 us
    ppermute x1, starting transfers between devices, on_device(): other = lax.ppermute(own.astype(jnp.bfloat16), 'wa', pairs(2, 1))  0.6 us
  transfers between devices with their start and end apart: 9, of which 7 were waited for; matrix products, arithmetic and copies ran while one was open for 3% of the time, Pallas kernels for 3%

profile of v1, /device:TPU:0, one launch (start us, length us, event | category | flops | bytes accessed | tf_op | source)
XLA Modules:
  0.0 26.7 jit_solution(15875741677532398611)
XLA Ops:
  0.6 1.9 %shard_map.59 = (bf16[2,2,64,128]{3,2,1,0:T(8,128)(2,1)S(1)}, bf16[2,2,2,4,64,128]{5,4,3,2,1,0:T(8,128)(2,1)S(1)}, bf16[2,2,4,64,128]{4,3,2,1,0:T(8,128)(2,1)S(1)}, s32[4,8,128]{2,1,0:T(8,128)S(1)}) custom-call(s32[1,4]{1,0:T(1,128)} %rows_far.1, bf16[2,2,2,1,4,64,128]{6,5,4,3,2,1,0:T(8,128)(2,1)} %field_far.1, bf16[2,2,4,64,128]{4,3,2,1,0:T(8,128)(2,1)} %kern_far.1), custom_call_target="tpu_custom_call" | custom-call | tf_op jit(solution)/shard_map/pallas_call | solution.py:226
  2.5 3.0 %collective-permute-start.1 = (bf16[2,2,64,128]{3,2,1,0:T(8,128)(2,1)S(1)}, bf16[2,2,64,128]{3,2,1,0:T(8,128)(2,1)S(1)}, u32[]{:S(2)}, u32[]{:S(2)}) collective-permute-start(bf16[2,2,64,128]{3,2,1,0:T(8,128)(2,1)S(1)} %get-tuple-element.22), channel_id=1, source_target_pairs={{0,2},{2,0},{1,3},{3,1},{4,6},{6,4},{5,7},{7,5},{8,10},{10,8},{9,1... | collective-permute-start | bytes 196616 | tf_op jit(solution)/shard_map/ppermute | solution.py:241
  5.5 0.5 %shard_map.60 = (bf16[2,256,128]{2,1,0:T(8,128)(2,1)S(1)}, bf16[2,4,128,256]{3,2,1,0:T(8,128)(2,1)S(1)}, bf16[2,4,128,128]{3,2,1,0:T(8,128)(2,1)S(1)}, bf16[2,2,...) custom-call(bf16[2,2,2,4,64,128]{5,4,3,2,1,0:T(8,128)(2,1)S(1)} %get-tuple-element.14.field, ...), custom_call_target="tpu_custom_call" | custom-call | tf_op jit(solution)/shard_map/pallas_call | solution.py:226
  6.0 0.0 copy-start
  6.1 0.1 collective-permute-start
  6.1 1.9 %collective-permute-done.1 = bf16[2,2,64,128]{3,2,1,0:T(8,128)(2,1)S(1)} collective-permute-done((bf16[2,2,64,128]{3,2,1,0:T(8,128)(2,1)S(1)}, bf16[2,2,64,128]{3,2,1,0:T(8,128)(2,1)S(1)}, u32[]{:S(2)}, u32[]{:S(2)}) %collective-permute-start.1) | collective-permute-done | bytes 65568 | tf_op jit(solution)/shard_map/ppermute | solution.py:241
  8.1 4.0 %collective-permute-start.2 = (bf16[2,2,64,128]{3,2,1,0:T(8,128)(2,1)S(1)}, bf16[2,2,64,128]{3,2,1,0:T(8,128)(2,1)S(1)}, u32[]{:S(2)}, u32[]{:S(2)}) collective-permute-start(bf16[2,2,64,128]{3,2,1,0:T(8,128)(2,1)S(1)} %add_convert_fusion.refs_5_), channel_id=1, source_target_pairs={{0,12},{4,8},{8,4},{12,0},{1,13},{5,9},{9,5},{13,1},{2,14},{6,10},... | collective-permute-start | bytes 196616 | tf_op jit(solution)/shard_map/ppermute | solution.py:241
  12.1 0.0 collective-permute-start.3
  12.1 0.6 %collective-permute-start.4 = (bf16[2,2,64,128]{3,2,1,0:T(8,128)(2,1)S(1)}, bf16[2,2,64,128]{3,2,1,0:T(8,128)(2,1)S(1)}, u32[]{:S(2)}, u32[]{:S(2)}) collective-permute-start(bf16[2,2,64,128]{3,2,1,0:T(8,128)(2,1)S(1)} %add_convert_fusion.refs_5_), channel_id=1, source_target_pairs={{0,4},{4,0},{8,12},{12,8},{1,5},{5,1},{9,13},{13,9},{2,6},{6,2},{1... | collective-permute-start | bytes 196616 | tf_op jit(solution)/shard_map/ppermute | solution.py:241
  12.8 1.7 %collective-permute-done.2.refs_2_ = bf16[2,2,64,128]{3,2,1,0:T(8,128)(2,1)S(1)} collective-permute-done((bf16[2,2,64,128]{3,2,1,0:T(8,128)(2,1)S(1)}, bf16[2,2,64,128]{3,2,1,0:T(8,128)(2,1)S(1)}, u32[]{:S(2)}, u32[]{:S(2)}) %collective-permute-start.2) | collective-permute-done | bytes 65568 | tf_op jit(solution)/shard_map/ppermute | solution.py:241
  14.4 2.8 %collective-permute-done.3.refs_3_ = bf16[2,2,64,128]{3,2,1,0:T(8,128)(2,1)S(1)} collective-permute-done((bf16[2,2,64,128]{3,2,1,0:T(8,128)(2,1)S(1)}, bf16[2,2,64,128]{3,2,1,0:T(8,128)(2,1)S(1)}, u32[]{:S(2)}, u32[]{:S(2)}) %collective-permute-start.3) | collective-permute-done | bytes 65568 | tf_op jit(solution)/shard_map/ppermute | solution.py:241
  17.3 0.0 collective-permute-done.4.refs_4_
  17.3 0.0 collective-permute-done.refs_1_
  17.3 0.0 copy-done
  17.3 1.7 %shard_map.61 = (f32[2,64,128]{2,1,0:T(8,128)S(1)}, bf16[2,128,256]{2,1,0:T(8,128)(2,1)S(1)}, bf16[4,64,128]{2,1,0:T(8,128)(2,1)S(1)}) custom-call(bf16[2,256,128]{2,1,0:T(8,128)(2,1)S(1)} %get-tuple-element.18.own_kern, bf16[2,4,128,128]{3,2,1,0:T(8,128)(2,1)S(1)} %get-tuple-element.19.strip_kern, f32[2,64,64]{2,1,0:T(8,128)S(1)} %copy-done, ...), custom_call_target="tpu_custom_call" | custom-call | tf_op jit(solution)/shard_map/pallas_call | solution.py:226
  19.1 0.1 collective-permute-start.7
  19.1 2.1 %collective-permute-start.6 = (bf16[64,128]{1,0:T(8,128)(2,1)S(1)}, bf16[64,128]{1,0:T(8,128)(2,1)S(1)}, u32[]{:S(2)}, u32[]{:S(2)}) collective-permute-start(bf16[64,128]{1,0:T(8,128)(2,1)S(1)} %get-tuple-element.28), channel_id=1, source_target_pairs={{0,8},{1,9},{4,12},{5,13},{8,0},{9,1},{12,4},{13,5},{2,10},{3,11},... | collective-permute-start | bytes 49160 | tf_op jit(solution)/shard_map/ppermute | solution.py:259
  21.2 1.7 %collective-permute-start.5 = (bf16[64,128]{1,0:T(8,128)(2,1)S(1)}, bf16[64,128]{1,0:T(8,128)(2,1)S(1)}, u32[]{:S(2)}, u32[]{:S(2)}) collective-permute-start(bf16[64,128]{1,0:T(8,128)(2,1)S(1)} %get-tuple-element.29), channel_id=1, source_target_pairs={{0,5},{1,4},{4,1},{5,0},{8,13},{9,12},{12,9},{13,8},{2,7},{3,6},{6... | collective-permute-start | bytes 49160 | tf_op jit(solution)/shard_map/ppermute | solution.py:259
  23.0 0.3 %shard_map.62 = f32[4,64,128]{2,1,0:T(8,128)S(1)} custom-call(bf16[2,2,2,4,64,128]{5,4,3,2,1,0:T(8,128)(2,1)S(1)} %get-tuple-element.14.field, s32[4,8,128]{2,1,0:T(8,128)S(1)} %get-tuple-element.15.counts, bf16[2,4,128,256]{3,2,1,0:T(8,128)(2,1)S(1)} %get-tuple-element.17.both_kern, bf16[2,128,256]{2,1,0:T(8,128)(2,1)S(1)} %get-tuple-element.23.sides), custom_call_target="tpu_custom_call" | custom-call | tf_op jit(solution)/shard_map/pallas_call | solution.py:226
  23.3 0.8 %collective-permute-done.7 = bf16[64,128]{1,0:T(8,128)(2,1)S(1)} collective-permute-done((bf16[64,128]{1,0:T(8,128)(2,1)S(1)}, bf16[64,128]{1,0:T(8,128)(2,1)S(1)}, u32[]{:S(2)}, u32[]{:S(2)}) %collective-permute-start.7) | collective-permute-done | bytes 16416 | tf_op jit(solution)/shard_map/ppermute | solution.py:259
  24.1 0.1 collective-permute-done.6
  24.2 0.2 collective-permute-done.5
  24.4 0.6 %collective-permute-start.8 = (bf16[4,64,128]{2,1,0:T(8,128)(2,1)S(1)}, bf16[4,64,128]{2,1,0:T(8,128)(2,1)S(1)}, u32[]{:S(2)}, u32[]{:S(2)}) collective-permute-start(bf16[4,64,128]{2,1,0:T(8,128)(2,1)S(1)} %fusion.1), channel_id=1, source_target_pairs={{0,1},{1,0},{2,3},{3,2},{4,5},{5,4},{6,7},{7,6},{8,9},{9,8},{10,11... | collective-permute-start | bytes 196616 | tf_op jit(solution)/shard_map/ppermute | solution.py:356
  25.0 0.7 %slice_add_fusion = f32[2,64,64]{2,1,0:T(8,128)} fusion(f32[2,64,128]{2,1,0:T(8,128)S(1)} %get-tuple-element.25), kind=kLoop, calls=%fused_computation.8 | loop fusion | flops 8192 | bytes 98304 | tf_op jit(solution)/shard_map/add | solution.py:358
  25.7 0.2 collective-permute-done.8
  26.0 0.7 %reverse_select_fusion = f32[1,2,2,64,128]{4,3,2,1,0:T(8,128)} fusion(f32[1,2,2,64,128]{4,3,2,1,0:T(8,128)S(1)} %fusion, pred[]{:T(512)S(6)} %ne.6), kind=kLoop, calls=%fused_computation | loop fusion | flops 32768 | bytes 262145 | tf_op jit(solution)/shard_map/jit(_where)/select_n | solution.py:279
  (5 shorter events, 0.1 us)
Async XLA Ops:
  2.5 5.5 %collective-permute-start.1 = (bf16[2,2,64,128]{3,2,1,0:T(8,128)(2,1)S(1)}, bf16[2,2,64,128]{3,2,1,0:T(8,128)(2,1)S(1)}, u32[]{:S(2)}, u32[]{:S(2)}) collective-permute-start(bf16[2,2,64,128]{3,2,1,0:T(8,128)(2,1)S(1)} %get-tuple-element.22), channel_id=1, source_target_pairs={{0,2},{2,0},{1,3},{3,1},{4,6},{6,4},{5,7},{7,5},{8,10},{10,8},{9,1... | collective-permute-start | bytes 196616 | tf_op jit(solution)/shard_map/ppermute | solution.py:241
  6.0 11.2 %copy-start = (f32[2,64,64]{2,1,0:T(8,128)S(1)}, f32[2,64,64]{2,1,0:T(8,128)}, u32[]{:S(2)}) copy-start(f32[2,64,64]{2,1,0:T(8,128)} %target.1) | copy-start | bytes 98308
  6.1 11.2 %collective-permute-start = (bf16[2,2,4,64,128]{4,3,2,1,0:T(8,128)(2,1)S(1)}, bf16[2,2,4,64,128]{4,3,2,1,0:T(8,128)(2,1)S(1)}, u32[]{:S(2)}, u32[]{:S(2)}) collective-permute-start(bf16[2,2,4,64,128]{4,3,2,1,0:T(8,128)(2,1)S(1)} %get-tuple-element.21), channel_id=1, source_target_pairs={{0,2},{2,0},{1,3},{3,1},{4,6},{6,4},{5,7},{7,5},{8,10},{10,8},{9,1... | collective-permute-start | bytes 786440 | tf_op jit(solution)/shard_map/ppermute | solution.py:241
  8.1 6.4 %collective-permute-start.2 = (bf16[2,2,64,128]{3,2,1,0:T(8,128)(2,1)S(1)}, bf16[2,2,64,128]{3,2,1,0:T(8,128)(2,1)S(1)}, u32[]{:S(2)}, u32[]{:S(2)}) collective-permute-start(bf16[2,2,64,128]{3,2,1,0:T(8,128)(2,1)S(1)} %add_convert_fusion.refs_5_), channel_id=1, source_target_pairs={{0,12},{4,8},{8,4},{12,0},{1,13},{5,9},{9,5},{13,1},{2,14},{6,10},... | collective-permute-start | bytes 196616 | tf_op jit(solution)/shard_map/ppermute | solution.py:241
  12.1 5.2 %collective-permute-start.3 = (bf16[2,2,64,128]{3,2,1,0:T(8,128)(2,1)S(1)}, bf16[2,2,64,128]{3,2,1,0:T(8,128)(2,1)S(1)}, u32[]{:S(2)}, u32[]{:S(2)}) collective-permute-start(bf16[2,2,64,128]{3,2,1,0:T(8,128)(2,1)S(1)} %add_convert_fusion.refs_5_), channel_id=1, source_target_pairs={{0,8},{4,12},{8,0},{12,4},{1,9},{5,13},{9,1},{13,5},{2,10},{6,14},... | collective-permute-start | bytes 196616 | tf_op jit(solution)/shard_map/ppermute | solution.py:241
  12.1 5.2 %collective-permute-start.4 = (bf16[2,2,64,128]{3,2,1,0:T(8,128)(2,1)S(1)}, bf16[2,2,64,128]{3,2,1,0:T(8,128)(2,1)S(1)}, u32[]{:S(2)}, u32[]{:S(2)}) collective-permute-start(bf16[2,2,64,128]{3,2,1,0:T(8,128)(2,1)S(1)} %add_convert_fusion.refs_5_), channel_id=1, source_target_pairs={{0,4},{4,0},{8,12},{12,8},{1,5},{5,1},{9,13},{13,9},{2,6},{6,2},{1... | collective-permute-start | bytes 196616 | tf_op jit(solution)/shard_map/ppermute | solution.py:241
  19.1 5.0 %collective-permute-start.7 = (bf16[64,128]{1,0:T(8,128)(2,1)S(1)}, bf16[64,128]{1,0:T(8,128)(2,1)S(1)}, u32[]{:S(2)}, u32[]{:S(2)}) collective-permute-start(bf16[64,128]{1,0:T(8,128)(2,1)S(1)} %get-tuple-element.27), channel_id=1, source_target_pairs={{0,13},{1,12},{4,9},{5,8},{8,5},{9,4},{12,1},{13,0},{2,15},{3,14},... | collective-permute-start | bytes 49160 | tf_op jit(solution)/shard_map/ppermute | solution.py:259
  19.1 5.0 %collective-permute-start.6 = (bf16[64,128]{1,0:T(8,128)(2,1)S(1)}, bf16[64,128]{1,0:T(8,128)(2,1)S(1)}, u32[]{:S(2)}, u32[]{:S(2)}) collective-permute-start(bf16[64,128]{1,0:T(8,128)(2,1)S(1)} %get-tuple-element.28), channel_id=1, source_target_pairs={{0,8},{1,9},{4,12},{5,13},{8,0},{9,1},{12,4},{13,5},{2,10},{3,11},... | collective-permute-start | bytes 49160 | tf_op jit(solution)/shard_map/ppermute | solution.py:259
  21.2 3.2 %collective-permute-start.5 = (bf16[64,128]{1,0:T(8,128)(2,1)S(1)}, bf16[64,128]{1,0:T(8,128)(2,1)S(1)}, u32[]{:S(2)}, u32[]{:S(2)}) collective-permute-start(bf16[64,128]{1,0:T(8,128)(2,1)S(1)} %get-tuple-element.29), channel_id=1, source_target_pairs={{0,5},{1,4},{4,1},{5,0},{8,13},{9,12},{12,9},{13,8},{2,7},{3,6},{6... | collective-permute-start | bytes 49160 | tf_op jit(solution)/shard_map/ppermute | solution.py:259
  24.4 1.5 %collective-permute-start.8 = (bf16[4,64,128]{2,1,0:T(8,128)(2,1)S(1)}, bf16[4,64,128]{2,1,0:T(8,128)(2,1)S(1)}, u32[]{:S(2)}, u32[]{:S(2)}) collective-permute-start(bf16[4,64,128]{2,1,0:T(8,128)(2,1)S(1)} %fusion.1), channel_id=1, source_target_pairs={{0,1},{1,0},{2,3},{3,2},{4,5},{5,4},{6,7},{7,6},{8,9},{9,8},{10,11... | collective-permute-start | bytes 196616 | tf_op jit(solution)/shard_map/ppermute | solution.py:356
